TPU v7x, 32 devices: a whole 2x2x4 slice. The times are simulated.
32 devices in a mesh: dp: 16 (over z, x, core), tensor: 2 (over y).
Axes of the slice: x: 2, y: 2, z: 4, core: 2. Of those that a mesh axis runs over, the one named last changes fastest.
Arguments:
- frames: bfloat16 [14336, 1024], P('dp'), may hold values from -6 to 6
- lengths: int32 [16], P('dp'), may hold values from 448 to 896, as said below
- span_starts: int32 [16, 58], P('dp'), may hold values from 0 to 886
- mask_embedding: bfloat16 [1024], replicated, may hold values from -6 to 6
- norm1_gain: bfloat16 [1024], replicated, may hold values from 0.5 to 1.5
- norm1_bias: bfloat16 [1024], replicated, may hold values from -1.796875 to 1.796875
- qkv_weight: bfloat16 [1024, 3, 1024], P(None, None, 'tensor'), may hold values from -0.25 to 0.25
- qv_bias: bfloat16 [2, 1024], P(None, 'tensor'), may hold values from -1.796875 to 1.796875
- out_weight: bfloat16 [1024, 1024], P('tensor'), may hold values from -0.75 to 0.75
- out_bias: bfloat16 [1024], replicated, may hold values from -1.796875 to 1.796875
- norm2_gain: bfloat16 [1024], replicated, may hold values from 0.5 to 1.5
- norm2_bias: bfloat16 [1024], replicated, may hold values from -1.796875 to 1.796875
- up_weight: bfloat16 [1024, 4096], P(None, 'tensor'), may hold values from -0.1875 to 0.1875
- up_bias: bfloat16 [4096], P('tensor'), may hold values from -1.796875 to 1.796875
- down_weight: bfloat16 [4096, 1024], P('tensor'), may hold values from -0.09375 to 0.09375
- down_bias: bfloat16 [1024], replicated, may hold values from -1.796875 to 1.796875
- head_weight: bfloat16 [1024, 32], replicated, may hold values from -0.1875 to 0.1875
- head_bias: bfloat16 [32], replicated, may hold values from -1.796875 to 1.796875
- logit_grad: bfloat16 [14336, 32], P('dp'), may hold values from -6 to 6
Outputs:
- logits: float32 [14336, 32], P('dp')
- frames_grad: float32 [14336, 1024], P('dp')
- mask_grad: float32 [1024], replicated
- norm1_gain_grad: float32 [1024], replicated
- norm1_bias_grad: float32 [1024], replicated
- qkv_grad: float32 [1024, 3, 1024], P(None, None, 'tensor')
- qv_bias_grad: float32 [2, 1024], P(None, 'tensor')
- out_grad: float32 [1024, 1024], P('tensor')
- out_bias_grad: float32 [1024], replicated
- norm2_gain_grad: float32 [1024], replicated
- norm2_bias_grad: float32 [1024], replicated
- up_grad: float32 [1024, 4096], P(None, 'tensor')
- up_bias_grad: float32 [4096], P('tensor')
- down_grad: float32 [4096, 1024], P('tensor')
- down_bias_grad: float32 [1024], replicated
- head_grad: float32 [1024, 32], replicated
- head_bias_grad: float32 [32], replicated
Inputs may be any that keep to these rules, and one draw needn't show every extreme that they name: Frames 0 to lengths - 1 of an utterance are valid; some utterance has all 896 frames valid.
All inputs are finite; a program needn't handle non-finite values.
Results may differ from a plain program's by a relative error of at most 0.02.
Values may be sent and summed in bfloat16 or wider, within the bound.
A program may use at most 256 MiB of HBM per device.

v0:
```python
from functools import partial

import jax
import jax.numpy as jnp
from jax import lax
from jax.sharding import PartitionSpec as P

HEAD_DIM = 64
MASK_SPAN = 10


EPS = 1e-05
NEG = -1e30


def norm_stats(row_block, gain, shift):
    center = row_block - jnp.mean(row_block, axis=-1, keepdims=True)
    spread = jnp.mean(center * center, axis=-1, keepdims=True)
    inverse = lax.rsqrt(spread + EPS)
    unit_rows = center * inverse
    return (unit_rows * gain + shift, unit_rows, inverse)


def norm_back(grad_rows, unit_rows, inverse, gain):
    grad_unit = grad_rows * gain
    first_mean = jnp.mean(grad_unit, axis=-1, keepdims=True)
    second_mean = jnp.mean(grad_unit * unit_rows, axis=-1, keepdims=True)
    return inverse * (grad_unit - first_mean - unit_rows * second_mean)


def masked_scores(queries, key_rows, key_valid):
    factor = HEAD_DIM ** (-0.5)
    scores = (
        jnp.einsum("qhd,khd->hqk", queries, key_rows, preferred_element_type=jnp.float32) * factor
    )
    return jnp.where(key_valid[None, None, :], scores, NEG)


def attend_forward(packed):
    queries, key_rows, values, key_valid = packed
    scores = masked_scores(queries, key_rows, key_valid)
    row_peak = jnp.max(scores, axis=-1, keepdims=True)
    exp_scores = jnp.exp(scores - row_peak)
    row_total = jnp.sum(exp_scores, axis=-1, keepdims=True)
    prob_rows = (exp_scores / row_total).astype(jnp.bfloat16)
    mixture = jnp.einsum("hqk,khd->qhd", prob_rows, values, preferred_element_type=jnp.float32)
    return (mixture, row_peak + jnp.log(row_total))


def attend_backward(packed):
    queries, key_rows, values, key_valid, log_total, grad_mixture = packed
    factor = HEAD_DIM ** (-0.5)
    scores = masked_scores(queries, key_rows, key_valid)
    prob_rows = jnp.exp(scores - log_total)
    grad_values = jnp.einsum(
        "hqk,qhd->khd",
        prob_rows.astype(jnp.bfloat16),
        grad_mixture,
        preferred_element_type=jnp.float32,
    )
    grad_probs = jnp.einsum(
        "qhd,khd->hqk", grad_mixture, values, preferred_element_type=jnp.float32
    )
    row_dot = jnp.sum(prob_rows * grad_probs, axis=-1, keepdims=True)
    grad_scores = (prob_rows * (grad_probs - row_dot)).astype(jnp.bfloat16)
    grad_queries = (
        jnp.einsum("hqk,khd->qhd", grad_scores, key_rows, preferred_element_type=jnp.float32)
        * factor
    )
    grad_keys = (
        jnp.einsum("hqk,qhd->khd", grad_scores, queries, preferred_element_type=jnp.float32)
        * factor
    )
    return (grad_queries, grad_keys, grad_values)


def local(
    frames,
    lengths,
    span_starts,
    mask_embedding,
    norm1_gain,
    norm1_bias,
    qkv_weight,
    qv_bias,
    out_weight,
    out_bias,
    norm2_gain,
    norm2_bias,
    up_weight,
    up_bias,
    down_weight,
    down_bias,
    head_weight,
    head_bias,
    logit_grad,
):
    utterances_here, span_count = span_starts.shape
    row_count, model_width = frames.shape
    frame_count = row_count // utterances_here
    local_width = qkv_weight.shape[2]
    heads_here = local_width // HEAD_DIM
    share_rows = row_count // lax.axis_size("tensor")
    share_start = lax.axis_index("tensor") * share_rows

    def own_rows(block):
        return lax.dynamic_slice_in_dim(block, share_start, share_rows, 0)

    places = jnp.arange(frame_count, dtype=jnp.int32)
    covered = (places[None, None, :] >= span_starts[:, :, None]) & (
        places[None, None, :] < span_starts[:, :, None] + MASK_SPAN
    )
    masked = jnp.any(covered, axis=1).reshape(row_count, 1)
    key_valid = places[None, :] < lengths[:, None]
    gain_one = norm1_gain.astype(jnp.float32)
    gain_two = norm2_gain.astype(jnp.float32)
    filled = jnp.where(
        masked, mask_embedding.astype(jnp.float32)[None, :], frames.astype(jnp.float32)
    )
    first_norm, first_unit, first_inverse = norm_stats(
        filled, gain_one, norm1_bias.astype(jnp.float32)
    )
    first_low = first_norm.astype(jnp.bfloat16)
    weight_flat = qkv_weight.reshape(model_width, 3 * local_width)
    bias_full = jnp.stack(
        [
            qv_bias[0].astype(jnp.float32),
            jnp.zeros((local_width,), jnp.float32),
            qv_bias[1].astype(jnp.float32),
        ]
    ).reshape(3 * local_width)
    projected = (
        jnp.dot(first_low, weight_flat, preferred_element_type=jnp.float32) + bias_full
    ).astype(jnp.bfloat16)
    triple = projected.reshape(utterances_here, frame_count, 3, heads_here, HEAD_DIM)
    queries = triple[:, :, 0]
    key_rows = triple[:, :, 1]
    values = triple[:, :, 2]
    mixture, log_total = lax.map(attend_forward, (queries, key_rows, values, key_valid))
    mixture_low = mixture.astype(jnp.bfloat16).reshape(row_count, local_width)
    hidden = own_rows(filled) + (
        lax.psum_scatter(
            jnp.dot(mixture_low, out_weight, preferred_element_type=jnp.float32),
            "tensor",
            scatter_dimension=0,
            tiled=True,
        )
        + out_bias.astype(jnp.float32)
    )
    second_norm, second_unit, second_inverse = norm_stats(
        hidden, gain_two, norm2_bias.astype(jnp.float32)
    )
    second_low = lax.all_gather(second_norm.astype(jnp.bfloat16), "tensor", axis=0, tiled=True)
    up_rows = jnp.dot(second_low, up_weight, preferred_element_type=jnp.float32) + up_bias.astype(
        jnp.float32
    )
    activ_low = jax.nn.gelu(up_rows, approximate=False).astype(jnp.bfloat16)
    output = hidden + (
        lax.psum_scatter(
            jnp.dot(activ_low, down_weight, preferred_element_type=jnp.float32).astype(
                jnp.bfloat16
            ),
            "tensor",
            scatter_dimension=0,
            tiled=True,
        ).astype(jnp.float32)
        + down_bias.astype(jnp.float32)
    )
    output_low = lax.all_gather(output.astype(jnp.bfloat16), "tensor", axis=0, tiled=True)
    logits = jnp.dot(
        output_low, head_weight, preferred_element_type=jnp.float32
    ) + head_bias.astype(jnp.float32)
    grad_output = jnp.einsum(
        "rv,dv->rd", logit_grad, head_weight, preferred_element_type=jnp.float32
    )
    head_grad = jnp.einsum("rd,rv->dv", output_low, logit_grad, preferred_element_type=jnp.float32)
    head_bias_grad = jnp.sum(logit_grad.astype(jnp.float32), axis=0)
    grad_branch = grad_output.astype(jnp.bfloat16)
    down_grad = jnp.einsum("rf,rd->fd", activ_low, grad_branch, preferred_element_type=jnp.float32)
    down_bias_grad = jnp.sum(grad_branch.astype(jnp.float32), axis=0)
    grad_activ = jnp.einsum(
        "rd,fd->rf", grad_branch, down_weight, preferred_element_type=jnp.float32
    )
    gelu_value, gelu_pull = jax.vjp(partial(jax.nn.gelu, approximate=False), up_rows)
    grad_up = gelu_pull(grad_activ)[0].astype(jnp.bfloat16)
    up_grad = jnp.einsum("rd,rf->df", second_low, grad_up, preferred_element_type=jnp.float32)
    up_bias_grad = jnp.sum(grad_up.astype(jnp.float32), axis=0)
    grad_second = lax.psum_scatter(
        jnp.einsum("rf,df->rd", grad_up, up_weight, preferred_element_type=jnp.float32),
        "tensor",
        scatter_dimension=0,
        tiled=True,
    )
    grad_output_here = own_rows(grad_output)
    norm2_gain_grad = jnp.sum(grad_second * second_unit, axis=0)
    norm2_bias_grad = jnp.sum(grad_second, axis=0)
    grad_hidden = grad_output_here + norm_back(grad_second, second_unit, second_inverse, gain_two)
    grad_attn = grad_hidden.astype(jnp.bfloat16)
    grad_attn = lax.all_gather(grad_attn, "tensor", axis=0, tiled=True)
    out_grad = jnp.einsum("rl,rd->ld", mixture_low, grad_attn, preferred_element_type=jnp.float32)
    out_bias_grad = jnp.sum(grad_attn.astype(jnp.float32), axis=0)
    grad_mixture = jnp.einsum(
        "rd,ld->rl", grad_attn, out_weight, preferred_element_type=jnp.float32
    ).astype(jnp.bfloat16)
    grad_mixture = grad_mixture.reshape(utterances_here, frame_count, heads_here, HEAD_DIM)
    grad_queries, grad_keys, grad_values = lax.map(
        attend_backward, (queries, key_rows, values, key_valid, log_total, grad_mixture)
    )
    grad_triple = (
        jnp.stack([grad_queries, grad_keys, grad_values], axis=2)
        .astype(jnp.bfloat16)
        .reshape(row_count, 3 * local_width)
    )
    qkv_grad = jnp.einsum(
        "rd,rc->dc", first_low, grad_triple, preferred_element_type=jnp.float32
    ).reshape(model_width, 3, local_width)
    column_sums = jnp.sum(grad_triple.astype(jnp.float32), axis=0).reshape(3, local_width)
    qv_bias_grad = jnp.stack([column_sums[0], column_sums[2]])
    grad_first = lax.psum_scatter(
        jnp.einsum(
            "rc,dc->rd", grad_triple, weight_flat, preferred_element_type=jnp.float32
        ).astype(jnp.bfloat16),
        "tensor",
        scatter_dimension=0,
        tiled=True,
    ).astype(jnp.float32)
    unit_here = own_rows(first_unit)
    inverse_here = own_rows(first_inverse)
    masked_here = own_rows(masked)
    norm1_gain_grad = jnp.sum(grad_first * unit_here, axis=0)
    norm1_bias_grad = jnp.sum(grad_first, axis=0)
    grad_filled = grad_hidden + norm_back(grad_first, unit_here, inverse_here, gain_one)
    frames_grad = jnp.where(masked_here, 0.0, grad_filled)
    mask_grad = jnp.sum(jnp.where(masked_here, grad_filled, 0.0), axis=0)
    (
        mask_grad,
        norm1_gain_grad,
        norm1_bias_grad,
        qkv_grad,
        qv_bias_grad,
        out_grad,
        out_bias_grad,
        norm2_gain_grad,
        norm2_bias_grad,
        up_grad,
        up_bias_grad,
        down_grad,
        down_bias_grad,
        head_grad,
        head_bias_grad,
    ) = (
        lax.psum(mask_grad.astype(jnp.bfloat16), "dp").astype(jnp.float32),
        lax.psum(norm1_gain_grad.astype(jnp.bfloat16), "dp").astype(jnp.float32),
        lax.psum(norm1_bias_grad.astype(jnp.bfloat16), "dp").astype(jnp.float32),
        lax.psum(qkv_grad.astype(jnp.bfloat16), "dp").astype(jnp.float32),
        lax.psum(qv_bias_grad.astype(jnp.bfloat16), "dp").astype(jnp.float32),
        lax.psum(out_grad.astype(jnp.bfloat16), "dp").astype(jnp.float32),
        lax.psum(out_bias_grad.astype(jnp.bfloat16), "dp").astype(jnp.float32),
        lax.psum(norm2_gain_grad.astype(jnp.bfloat16), "dp").astype(jnp.float32),
        lax.psum(norm2_bias_grad.astype(jnp.bfloat16), "dp").astype(jnp.float32),
        lax.psum(up_grad.astype(jnp.bfloat16), "dp").astype(jnp.float32),
        lax.psum(up_bias_grad.astype(jnp.bfloat16), "dp").astype(jnp.float32),
        lax.psum(down_grad.astype(jnp.bfloat16), "dp").astype(jnp.float32),
        lax.psum(down_bias_grad.astype(jnp.bfloat16), "dp").astype(jnp.float32),
        lax.psum(head_grad.astype(jnp.bfloat16), "dp").astype(jnp.float32),
        lax.psum(head_bias_grad.astype(jnp.bfloat16), "dp").astype(jnp.float32),
    )
    frames_grad = lax.all_gather(
        frames_grad.astype(jnp.bfloat16), "tensor", axis=0, tiled=True
    ).astype(frames_grad.dtype)
    mask_grad, norm1_gain_grad, norm1_bias_grad, norm2_gain_grad, norm2_bias_grad = lax.psum(
        (mask_grad, norm1_gain_grad, norm1_bias_grad, norm2_gain_grad, norm2_bias_grad), "tensor"
    )
    return (
        logits,
        frames_grad,
        mask_grad,
        norm1_gain_grad,
        norm1_bias_grad,
        qkv_grad,
        qv_bias_grad,
        out_grad,
        out_bias_grad,
        norm2_gain_grad,
        norm2_bias_grad,
        up_grad,
        up_bias_grad,
        down_grad,
        down_bias_grad,
        head_grad,
        head_bias_grad,
    )


def solution(mesh):
    placed = (
        P("dp", None),
        P("dp"),
        P("dp", None),
        P(),
        P(),
        P(),
        P(None, None, "tensor"),
        P(None, "tensor"),
        P("tensor", None),
        P(),
        P(),
        P(),
        P(None, "tensor"),
        P("tensor"),
        P("tensor", None),
        P(),
        P(),
        P(),
        P("dp", None),
    )
    return jax.shard_map(
        local,
        mesh=mesh,
        in_specs=placed,
        out_specs=(
            P("dp", None),
            P("dp", None),
            P(),
            P(),
            P(),
            P(None, None, "tensor"),
            P(None, "tensor"),
            P("tensor", None),
            P(),
            P(),
            P(),
            P(None, "tensor"),
            P("tensor"),
            P("tensor", None),
            P(),
            P(),
            P(),
        ),
        check_vma=False,
    )
```

profile of v0, /device:TPU:0, one launch (start us, length us, event | category | flops | bytes accessed | tf_op | source)
XLA Modules:
  0.0 757.3 jit_solution(10334725320418066629)
XLA Ops:
  11.5 2.0 fusion.15
  13.6 2.4 multiply_reduce_fusion.1
  16.3 4.7 copy.51
  21.0 6.8 add_convert_fusion.1
  27.8 4.5 copy.52
  32.3 14.5 %fusion.40 = (f32[8,896]{1,0:T(8,128)S(1)}, f32[8,896,896]{1,2,0:T(8,128)}) fusion(bf16[1,896,3,8,64]{1,4,3,2,0:T(8,128)(2,1)} %bitcast.79, pred[896]{0:T(1024)(128)(4,1)S(1)} %iota_compare_fusion.2), kind=kOutput, calls=%fused_computation.101 | convolution fusion | flops 841344000 | bytes 27554688 | tf_op jit(solution)/shard_map/while/body/eval_jaxpr/qhd,khd->hqk/dot_general | solution.py:34
  46.7 10.6 %fusion = f32[8,896]{1,0:T(8,128)S(1)} fusion(f32[8,896,896]{1,2,0:T(8,128)} %get-tuple-element.113, f32[8,896]{1,0:T(8,128)S(1)} %get-tuple-element.112), kind=kLoop, calls=%fused_computation.6 | loop fusion | flops 12837888 | bytes 25747456 | tf_op jit(solution)/shard_map/while/body/eval_jaxpr/reduce_sum | solution.py:44
  57.4 13.2 %fusion.25 = bf16[8,64,896]{2,1,0:T(8,128)(2,1)S(1)} fusion(f32[8,896,896]{1,2,0:T(8,128)} %get-tuple-element.113, f32[8,896]{1,0:T(8,128)S(1)} %fusion, f32[8,896]{1,0:T(8,128)S(1)} %get-tuple-element.112, bf16[1,896,3,8,64]{1,4,3,2,0:T(8,128)(2,1)} %bitcast.80), kind=kOutput, calls=%fused_computation.67 | convolution fusion | flops 841809920 | bytes 27582464 | tf_op jit(solution)/shard_map/while/body/eval_jaxpr/hqk,khd->qhd/dot_general | solution.py:46
  71.5 3.0 fusion.42
  74.7 3.5 subtract_multiply_fusion
  78.2 48.3 %reduce-scatter.5.cloned.1.call-done = f32[448,1024]{1,0:T(8,128)} async-done(((f32[896,1024]{1,0:T(8,128)}), f32[448,1024]{1,0:T(8,128)}) %reduce-scatter.5.cloned.1.call-update) | async-done | bytes 1835024 | tf_op jit(solution)/shard_map/reduce_scatter | solution.py:142
  126.5 2.3 fusion.38
  130.6 3.0 convert_reduce_fusion
  133.7 27.2 %all-gather.5.cloned.1.call-done = bf16[896,1024]{1,0:T(8,128)(2,1)} async-done(((bf16[448,1024]{1,0:T(8,128)(2,1)}), bf16[896,1024]{1,0:T(8,128)(2,1)}) %all-gather.5.cloned.1.call-update) | async-done | bytes 1835024 | tf_op jit(solution)/shard_map/all_gather | solution.py:153
  160.9 24.0 %multiply_convert_fusion.1 = (bf16[896,2048]{1,0:T(8,128)(2,1)}, f32[896,2048]{1,0:T(8,128)}, f32[896,2048]{1,0:T(8,128)}) fusion(f32[2048]{0:T(1024)S(1)} %convert_element_type.235, bf16[896,1024]{1,0:T(8,128)(2,1)} %all-gather.5.cloned.1.call-done, bf16[1024,2048]{1,0:T(8,128)(2,1)} %param.31), kind=kOutput, calls=%fused_computation.14 | convolution fusion | flops 3879206912 | bytes 24387584 | tf_op jit(solution)/shard_map/dot_general | solution.py:154
  184.9 9.9 %fusion.41 = (bf16[2048]{0:T(1024)(128)(2,1)S(1)}, bf16[896,2048]{1,0:T(8,128)(2,1)S(1)}) fusion(f32[896,2048]{1,0:T(8,128)} %get-tuple-element.102, bf16[2048,1024]{1,0:T(8,128)(2,1)S(1)} %copy-done.39, f32[896,1024]{1,0:T(8,128)S(1)} %copy-done.4, f32[896,2048]{1,0:T(8,128)} %get-tuple-element.114, f32[2048]{0:T(1024)S(1)} %convert_element_type.235), kind=kOutput, calls=%fused_computation.102 | convolution fusion | flops 3788371968 | bytes 26226688 | tf_op jit(solution)/shard_map/rd,fd->rf/dot_general | solution.py:181
  196.6 5.8 fusion.43
  202.7 8.5 %convolution_convert_fusion.4 = bf16[896,1024]{1,0:T(8,128)(2,1)} fusion(bf16[896,2048]{1,0:T(8,128)(2,1)} %get-tuple-element.101, bf16[2048,1024]{1,0:T(8,128)(2,1)} %param.33), kind=kOutput, calls=%fused_computation.61 | convolution fusion | flops 3759013888 | bytes 9699328 | tf_op jit(solution)/shard_map/dot_general | solution.py:160
  211.3 40.4 %reduce-scatter.9.cloned.1.call-done = f32[448,1024]{1,0:T(8,128)} async-done(((f32[896,1024]{1,0:T(8,128)}), f32[448,1024]{1,0:T(8,128)}) %reduce-scatter.9.cloned.1.call-update) | async-done | bytes 1835024 | tf_op jit(solution)/shard_map/reduce_scatter | solution.py:188
  251.8 2.3 multiply_reduce_fusion.2
  254.1 29.3 %reduce-scatter.7.cloned.1.call-done = bf16[448,1024]{1,0:T(8,128)(2,1)} async-done(((bf16[896,1024]{1,0:T(8,128)(2,1)}), bf16[448,1024]{1,0:T(8,128)(2,1)}) %reduce-scatter.7.cloned.1.call-update) | async-done | bytes 917520 | tf_op jit(solution)/shard_map/reduce_scatter | solution.py:159
  283.4 4.9 fusion.36
  288.4 30.2 %all-gather.9.cloned.1.call-done = bf16[896,1024]{1,0:T(8,128)(2,1)} async-done(((bf16[448,1024]{1,0:T(8,128)(2,1)}), bf16[896,1024]{1,0:T(8,128)(2,1)}) %all-gather.9.cloned.1.call-update) | async-done | bytes 1835024 | tf_op jit(solution)/shard_map/all_gather | solution.py:199
  318.7 2.8 convolution_convert_fusion.6
  321.5 12.5 %fusion.22 = bf16[1,896,1,8,64]{1,4,3,2,0:T(8,128)(2,1)S(1)} fusion(bf16[896,8,64]{0,2,1:T(8,128)(2,1)S(1)} %bitcast.84, f32[8,896,896]{1,2,0:T(8,128)} %get-tuple-element.113, f32[8,896]{1,0:T(8,128)S(1)} %log_add_fusion), kind=kOutput, calls=%fused_computation.64 | convolution fusion | flops 834928640 | bytes 27553792 | tf_op jit(solution)/shard_map/while/body/eval_jaxpr/hqk,qhd->khd/dot_general | solution.py:55
  334.0 16.8 %multiply_reduce_fusion = (f32[8,896]{1,0:T(8,128)S(1)}, f32[8,896,896]{1,2,0:T(8,128)}) fusion(f32[8,896,896]{1,2,0:T(8,128)} %get-tuple-element.113, f32[8,896]{1,0:T(8,128)S(1)} %log_add_fusion, bf16[896,8,64]{0,2,1:T(8,128)(2,1)S(1)} %bitcast.85, bf16[1,896,3,8,64]{1,4,3,2,0:T(8,128)(2,1)} %bitcast.81), kind=kOutput, calls=%fused_computation.1 | convolution fusion | flops 841344000 | bytes 53272576 | tf_op jit(solution)/shard_map/while/body/eval_jaxpr/qhd,khd->hqk/dot_general | solution.py:61
  350.8 22.2 %multiply_convert_fusion = bf16[8,896,896]{1,2,0:T(8,128)(2,1)} fusion(f32[8,896,896]{1,2,0:T(8,128)} %get-tuple-element.116, f32[8,896,896]{1,2,0:T(8,128)} %get-tuple-element.113, f32[8,896]{1,0:T(8,128)S(1)} %get-tuple-element.115, f32[8,896]{1,0:T(8,128)S(1)} %log_add_fusion), kind=kLoop, calls=%fused_computation | loop fusion | flops 25690112 | bytes 64282624 | tf_op jit(solution)/shard_map/while/body/eval_jaxpr/convert_element_type | solution.py:65
  373.0 8.7 %multiply_bitcast_fusion = bf16[1,896,1,8,64]{1,4,3,2,0:T(8,128)(2,1)S(1)} fusion(bf16[8,896,896]{1,2,0:T(8,128)(2,1)} %multiply_convert_fusion, bf16[1,896,3,8,64]{1,4,3,2,0:T(8,128)(2,1)S(1)} %bitcast.82), kind=kOutput, calls=%fused_computation.52 | convolution fusion | flops 823001088 | bytes 14680064 | tf_op jit(solution)/shard_map/while/body/eval_jaxpr/hqk,qhd->khd/dot_general | solution.py:71
  381.7 6.8 multiply_bitcast_fusion.1
  391.4 4.2 convolution_convert_fusion.3
  396.7 9.7 %convolution_convert_fusion = bf16[2048,1024]{1,0:T(8,128)(2,1)} fusion(bf16[896,2048]{1,0:T(8,128)(2,1)} %get-tuple-element.101, f32[896,1024]{1,0:T(8,128)} %get-tuple-element.120), kind=kOutput, calls=%fused_computation.30 | convolution fusion | flops 3761111040 | bytes 11534336 | tf_op jit(solution)/shard_map/rf,rd->fd/dot_general | solution.py:179
  406.4 18.3 %reduce-scatter.11.cloned.1.call-done = bf16[448,1024]{1,0:T(8,128)(2,1)} async-done(((bf16[896,1024]{1,0:T(8,128)(2,1)}), bf16[448,1024]{1,0:T(8,128)(2,1)}) %reduce-scatter.11.cloned.1.call-update) | async-done | bytes 917520 | tf_op jit(solution)/shard_map/reduce_scatter | solution.py:219
  424.7 2.4 fusion.20
  427.2 2.4 select_reduce_fusion
  431.3 9.8 %convolution_convert_fusion.1 = bf16[1024,2048]{1,0:T(8,128)(2,1)} fusion(bf16[896,1024]{1,0:T(8,128)(2,1)} %all-gather.5.cloned.1.call-done, bf16[896,2048]{1,0:T(8,128)(2,1)} %copy-done.41), kind=kOutput, calls=%fused_computation.31 | convolution fusion | flops 3760193536 | bytes 9699328 | tf_op jit(solution)/shard_map/rd,rf->df/dot_general | solution.py:186
  441.1 15.4 %all-gather.7.cloned.1.call-done = bf16[896,1024]{1,0:T(8,128)(2,1)} async-done(((bf16[448,1024]{1,0:T(8,128)(2,1)}), bf16[896,1024]{1,0:T(8,128)(2,1)}) %all-gather.7.cloned.1.call-update) | async-done | bytes 1835024 | tf_op jit(solution)/shard_map/all_gather | solution.py:169
  456.5 2.6 convolution_convert_fusion.7
  459.1 3.6 convolution_convert_fusion.5
  462.7 5.8 convolution_convert_fusion.2
  471.3 2.8 convolution_add_fusion
  474.3 63.4 %all-reduce.1 = (bf16[1024]{0:T(1024)(128)(2,1)S(1)}, bf16[1024]{0:T(1024)(128)(2,1)S(1)}, bf16[1024]{0:T(1024)(128)(2,1)S(1)}, bf16[1024]{0:T(1024)(128)(2,1)S(...) all-reduce(bf16[1024]{0:T(1024)(128)(2,1)S(1)} %get-tuple-element.9, ...), channel_id=1, replica_groups=mesh['dp'=16,'tensor'=2] {'dp'}, use_global_device_ids=true, to_apply=%region_17.18 | all-reduce | flops 10272 | bytes 41088 | tf_op jit(solution)/shard_map/psum | solution.py:252
  540.6 8.1 %all-reduce = (f32[1024]{0:T(1024)}, f32[1024]{0:T(1024)}, f32[1024]{0:T(1024)}, f32[1024]{0:T(1024)}, f32[1024]{0:T(1024)}) all-reduce(bf16[1024]{0:T(1024)(128)(2,1)S(1)} %get-tuple-element.80, bf16[1024]{0:T(1024)(128)(2,1)S(1)} %get-tuple-element.81, ...), channel_id=1, replica_groups=mesh['dp'=16,'tensor'=2] {'tensor'}, use_global_device_ids=true, to_apply=%region_18.19 | all-reduce | flops 5120 | bytes 30720 | tf_op jit(solution)/shard_map/psum | solution.py:271
  548.7 3.8 convert_element_type.253
  552.5 181.1 %all-reduce.5.cloned.1.call-done = (bf16[1024,3,512]{2,0,1:T(8,128)(2,1)}, bf16[512,1024]{1,0:T(8,128)(2,1)}, bf16[1024,2048]{1,0:T(8,128)(2,1)}, bf16[2048,1024]{1,0:T(8,128)(2,1)}, bf16[1024,32]{0,1:T(8,128)(2,1)}) async-done(((bf16[1024,3,512]{2,0,1:T(8,128)(2,1)}, bf16[512,1024]{1,0:T(8,128)(2,1)}, bf16[1024,2048]{1,0:T(8,128)(2,1)}, bf16[2048,1024]{1,0:T(8,128)(2,1)}, bf16[1024,32]{0,1:T(8,128)(2,1)}), ...) | async-done | bytes 12648464 | tf_op jit(solution)/shard_map/psum | solution.py:255
  735.3 2.8 convert_element_type.264
  738.1 3.6 convert_element_type.260
  741.7 4.4 convert_element_type.271
  746.1 4.4 convert_element_type.274
  (146 shorter events, 21.9 us)
Async XLA Ops:
  7.2 64.3 %copy-start = (bf16[512,1024]{1,0:T(8,128)(2,1)S(1)}, bf16[512,1024]{1,0:T(8,128)(2,1)}, u32[]{:S(2)}) copy-start(bf16[512,1024]{1,0:T(8,128)(2,1)} %param.27) | copy-start | bytes 3145732
  7.2 8.9 %copy-start.30 = (bf16[2,512]{1,0:T(2,128)(2,1)S(1)}, bf16[2,512]{1,0:T(2,128)(2,1)}, u32[]{:S(2)}) copy-start(bf16[2,512]{1,0:T(2,128)(2,1)} %param.26) | copy-start | bytes 6148
  7.2 119.3 %reduce-scatter.5.cloned.1.call-start = ((), (), s32[]{:S(2)}) async-start(), calls=%async_computation.4 | async-start | bytes 5505024 | tf_op jit(solution)/shard_map/reduce_scatter | solution.py:142
  9.3 65.3 %copy-start.19 = (f32[1024]{0:T(1024)}, f32[1024]{0:T(1024)S(1)}, u32[]{:S(2)}) copy-start(f32[1024]{0:T(1024)S(1)} %convert_element_type.220) | copy-start | bytes 12292
  10.0 11.0 %copy-start.23 = (f32[1024]{0:T(1024)}, f32[1024]{0:T(1024)S(1)}, u32[]{:S(2)}) copy-start(f32[1024]{0:T(1024)S(1)} %convert_element_type.222) | copy-start | bytes 12292
  10.7 10.3 %copy-start.32 = (f32[1024]{0:T(1024)}, f32[1024]{0:T(1024)S(1)}, u32[]{:S(2)}) copy-start(f32[1024]{0:T(1024)S(1)} %convert_element_type.223) | copy-start | bytes 12292
  11.5 63.2 %copy-start.27 = (pred[896]{0:T(1024)(128)(4,1)}, pred[896]{0:T(1024)(128)(4,1)S(1)}, u32[]{:S(2)}) copy-start(pred[896]{0:T(1024)(128)(4,1)S(1)} %fusion.28) | copy-start | bytes 2692
  13.6 61.1 %copy-start.21 = (f32[896]{0:T(1024)}, f32[896]{0:T(1024)S(1)}, u32[]{:S(2)}) copy-start(f32[896]{0:T(1024)S(1)} %broadcast_multiply_fusion) | copy-start | bytes 10756
  13.6 7.4 copy-start.2
  16.1 58.6 %copy-start.25 = (f32[896]{0:T(1024)}, f32[896]{0:T(1024)S(1)}, u32[]{:S(2)}) copy-start(f32[896]{0:T(1024)S(1)} %add_rsqrt_fusion) | copy-start | bytes 10756
  71.5 3.1 copy-start.34
  71.5 3.1 copy-start.35
  71.5 3.1 copy-start.36
  74.6 86.3 %all-gather.5.cloned.1.call-start = ((), (), s32[]{:S(2)}) async-start(), calls=%async_computation.5 | async-start | bytes 2752512 | tf_op jit(solution)/shard_map/all_gather | solution.py:153
  128.8 1.8 copy-start.31
  128.9 1.8 copy-start.15
  128.9 1.8 copy-start.17
  130.6 121.2 %reduce-scatter.9.cloned.1.call-start = ((), (), s32[]{:S(2)}) async-start(), calls=%async_computation.8 | async-start | bytes 5505024 | tf_op jit(solution)/shard_map/reduce_scatter | solution.py:188
  160.9 24.0 %copy-start.4 = (f32[896,1024]{1,0:T(8,128)S(1)}, f32[896,1024]{1,0:T(8,128)}, u32[]{:S(2)}) copy-start(f32[896,1024]{1,0:T(8,128)} %get-tuple-element.120) | copy-start | bytes 11010052
  160.9 24.0 %copy-start.39 = (bf16[2048,1024]{1,0:T(8,128)(2,1)S(1)}, bf16[2048,1024]{1,0:T(8,128)(2,1)}, u32[]{:S(2)}) copy-start(bf16[2048,1024]{1,0:T(8,128)(2,1)} %param.33) | copy-start | bytes 12582916
  184.9 11.7 %copy-start.38 = (bf16[1024,2048]{1,0:T(8,128)(2,1)S(1)}, bf16[1024,2048]{1,0:T(8,128)(2,1)}, u32[]{:S(2)}) copy-start(bf16[1024,2048]{1,0:T(8,128)(2,1)} %param.31) | copy-start | bytes 12582916
  194.8 1.8 copy-start.41
  202.5 80.9 %reduce-scatter.7.cloned.1.call-start = ((), (), s32[]{:S(2)}) async-start(), calls=%async_computation.6 | async-start | bytes 2752512 | tf_op jit(solution)/shard_map/reduce_scatter | solution.py:159
  202.7 8.6 %copy-start.37 = (bf16[1024]{0:T(1024)(128)(2,1)S(1)}, bf16[1024]{0:T(1024)(128)(2,1)}, u32[]{:S(2)}) copy-start(bf16[1024]{0:T(1024)(128)(2,1)} %param.34) | copy-start | bytes 6148
  211.2 107.5 %all-gather.9.cloned.1.call-start = ((), (), s32[]{:S(2)}) async-start(), calls=%async_computation.9 | async-start | bytes 2752512 | tf_op jit(solution)/shard_map/all_gather | solution.py:199
  288.4 136.3 %reduce-scatter.11.cloned.1.call-start = ((), (), s32[]{:S(2)}) async-start(), calls=%async_computation.10 | async-start | bytes 2752512 | tf_op jit(solution)/shard_map/reduce_scatter | solution.py:219
  350.8 22.2 %copy-start.1 = (bf16[896,1536]{0,1:T(8,128)(2,1)S(1)}, bf16[896,1536]{0,1:T(8,128)(2,1)}, u32[]{:S(2)}) copy-start(bf16[896,1536]{0,1:T(8,128)(2,1)} %copy.52) | copy-start | bytes 8257540
  388.5 2.9 copy-start.9
  391.4 4.3 copy-start.28
  391.4 4.4 copy-start.26
  395.6 60.8 %all-gather.7.cloned.1.call-start = ((), (), s32[]{:S(2)}) async-start(), calls=%async_computation.7 | async-start | bytes 2752512 | tf_op jit(solution)/shard_map/all_gather | solution.py:169
  396.4 28.3 %copy-start.24 = (f32[1024]{0:T(1024)S(1)}, f32[1024]{0:T(1024)}, u32[]{:S(2)}) copy-start(f32[1024]{0:T(1024)} %copy-done.23) | copy-start | bytes 12292
  396.4 152.3 %all-gather.11.cloned.1.call-start = ((), (), s32[]{:S(2)}) async-start(), calls=%async_computation.11 | async-start | bytes 2752512 | tf_op jit(solution)/shard_map/all_gather | solution.py:268
  406.4 20.8 %copy-start.6 = (f32[448,1024]{1,0:T(8,128)S(1)}, f32[448,1024]{1,0:T(8,128)}, u32[]{:S(2)}) copy-start(f32[448,1024]{1,0:T(8,128)} %get-tuple-element.100) | copy-start | bytes 5505028
  430.8 25.7 %copy-start.16 = (bf16[896,32]{0,1:T(8,128)(2,1)S(1)}, bf16[896,32]{0,1:T(8,128)(2,1)}, u32[]{:S(2)}) copy-start(bf16[896,32]{0,1:T(8,128)(2,1)} %param.37) | copy-start | bytes 172036
  430.8 28.3 %copy-start.13 = (bf16[896,1024]{1,0:T(8,128)(2,1)S(1)}, bf16[896,1024]{1,0:T(8,128)(2,1)}, u32[]{:S(2)}) copy-start(bf16[896,1024]{1,0:T(8,128)(2,1)} %all-gather.9.cloned.1.call-done) | copy-start | bytes 5505028
  430.8 302.8 %all-reduce.5.cloned.1.call-start = ((), (), s32[]{:S(2)}) async-start(), calls=%async_computation.12 | async-start | bytes 25296896 | tf_op jit(solution)/shard_map/psum | solution.py:255
  459.0 3.6 copy-start.3
  459.0 3.6 copy-start.12
  459.0 3.6 copy-start.20
  459.0 3.6 copy-start.22
  459.1 3.6 copy-start.33
  468.5 2.8 copy-start.18
  469.1 4.9 copy-start.5
  469.1 5.1 copy-start.29
  733.6 4.4 copy-start.10
  738.1 3.6 copy-start.8
  741.7 4.5 copy-start.7
  (3 other events, 3.1 us)
Sparse Core Ops, SparseCore 0:
  74.7 51.7 reduce-scatter.4
  130.7 30.1 all-gather.4
  202.6 49.0 reduce-scatter.8
  254.4 28.9 reduce-scatter.6
  288.5 30.1 all-gather.8
  395.7 28.9 reduce-scatter.10
  426.3 30.1 all-gather.6
  458.6 30.1 all-gather.10
  494.9 238.6 all-reduce.4
where the time goes:
time: 765 us; the launch traced here: 757 us
  waiting for transfers between devices  391 us (51%)
  matrix products  175 us (23%)
  other arithmetic  87.8 us (11%)
  blocking collectives  71.6 us (9%)
  local copies, waits for them, and re-layouts  15.6 us (2%)
  between operations  15.3 us (2%)
    psum x1, waiting for transfers between devices, local(): lax.psum(qkv_grad.astype(jnp.bfloat16), 'dp').astype(jnp.float32)  181 us
    psum x1, blocking collectives, local(): lax.psum(mask_grad.astype(jnp.bfloat16), 'dp').astype(jnp.float32)  63.4 us
    reduce_scatter x1, waiting for transfers between devices, local(): lax.psum_scatter(jnp.dot(mixture_low, out_weight, preferred_element_type=...  48.3 us
    reduce_scatter x1, waiting for transfers between devices, local(): lax.psum_scatter(jnp.einsum('rf,df->rd', grad_up, up_weight, preferred_el...  40.4 us
    all_gather x1, waiting for transfers between devices, local(): grad_attn = lax.all_gather(grad_attn, 'tensor', axis=0, tiled=True)  30.2 us
    reduce_scatter x1, waiting for transfers between devices, local(): lax.psum_scatter(jnp.dot(activ_low, down_weight, preferred_element_type=j...  29.3 us
    all_gather x1, waiting for transfers between devices, local(): lax.all_gather(second_norm.astype(jnp.bfloat16), 'tensor', axis=0, tiled=...  27.2 us
    dot_general x1, matrix products, local(): jnp.dot(second_low, up_weight, preferred_element_type=jnp.float32)  24 us
  transfers between devices with their start and end apart: 9, of which 8 were waited for; matrix products, arithmetic and copies ran while one was open for 9% of the time, Pallas kernels for 0%

commit v1 on v0

v1 whole, which is shorter than its diff:
```python
from functools import partial

import jax
import jax.numpy as jnp
from jax import lax
from jax.sharding import PartitionSpec as P

HEAD_DIM = 64
MASK_SPAN = 10


EPS = 1e-05
NEG = -1e30


def norm_stats(row_block, gain, shift):
    center = row_block - jnp.mean(row_block, axis=-1, keepdims=True)
    spread = jnp.mean(center * center, axis=-1, keepdims=True)
    inverse = lax.rsqrt(spread + EPS)
    unit_rows = center * inverse
    return (unit_rows * gain + shift, unit_rows, inverse)


def norm_back(grad_rows, unit_rows, inverse, gain):
    grad_unit = grad_rows * gain
    first_mean = jnp.mean(grad_unit, axis=-1, keepdims=True)
    second_mean = jnp.mean(grad_unit * unit_rows, axis=-1, keepdims=True)
    return inverse * (grad_unit - first_mean - unit_rows * second_mean)


def masked_scores(queries, key_rows, key_valid):
    factor = HEAD_DIM ** (-0.5)
    scores = (
        jnp.einsum("qhd,khd->hqk", queries, key_rows, preferred_element_type=jnp.float32) * factor
    )
    return jnp.where(key_valid[None, None, :], scores, NEG)


def attend_forward(packed):
    queries, key_rows, values, key_valid = packed
    scores = masked_scores(queries, key_rows, key_valid)
    row_peak = jnp.max(scores, axis=-1, keepdims=True)
    exp_scores = jnp.exp(scores - row_peak)
    row_total = jnp.sum(exp_scores, axis=-1, keepdims=True)
    prob_rows = (exp_scores / row_total).astype(jnp.bfloat16)
    mixture = jnp.einsum("hqk,khd->qhd", prob_rows, values, preferred_element_type=jnp.float32)
    return (mixture, row_peak + jnp.log(row_total))


def attend_backward(packed):
    queries, key_rows, values, key_valid, log_total, grad_mixture = packed
    factor = HEAD_DIM ** (-0.5)
    scores = masked_scores(queries, key_rows, key_valid)
    prob_rows = jnp.exp(scores - log_total)
    grad_values = jnp.einsum(
        "hqk,qhd->khd",
        prob_rows.astype(jnp.bfloat16),
        grad_mixture,
        preferred_element_type=jnp.float32,
    )
    grad_probs = jnp.einsum(
        "qhd,khd->hqk", grad_mixture, values, preferred_element_type=jnp.float32
    )
    row_dot = jnp.sum(prob_rows * grad_probs, axis=-1, keepdims=True)
    grad_scores = (prob_rows * (grad_probs - row_dot)).astype(jnp.bfloat16)
    grad_queries = (
        jnp.einsum("hqk,khd->qhd", grad_scores, key_rows, preferred_element_type=jnp.float32)
        * factor
    )
    grad_keys = (
        jnp.einsum("hqk,qhd->khd", grad_scores, queries, preferred_element_type=jnp.float32)
        * factor
    )
    return (grad_queries, grad_keys, grad_values)


def local(
    frames,
    lengths,
    span_starts,
    mask_embedding,
    norm1_gain,
    norm1_bias,
    qkv_weight,
    qv_bias,
    out_weight,
    out_bias,
    norm2_gain,
    norm2_bias,
    up_weight,
    up_bias,
    down_weight,
    down_bias,
    head_weight,
    head_bias,
    logit_grad,
):
    utterances_here, span_count = span_starts.shape
    row_count, model_width = frames.shape
    frame_count = row_count // utterances_here
    local_width = qkv_weight.shape[2]
    heads_here = local_width // HEAD_DIM
    f32, bf16 = jnp.float32, jnp.bfloat16
    first_share = lax.axis_index("tensor") == 0

    def mm(spec, left, right):
        return jnp.einsum(spec, left, right, preferred_element_type=f32)

    def split(wide):
        high = wide.astype(bf16)
        return jnp.concatenate([high, (wide - high.astype(f32)).astype(bf16)], axis=-1)

    places = jnp.arange(frame_count, dtype=jnp.int32)
    covered = (places[None, None, :] >= span_starts[:, :, None]) & (
        places[None, None, :] < span_starts[:, :, None] + MASK_SPAN
    )
    masked = jnp.any(covered, axis=1).reshape(row_count, 1)
    key_valid = places[None, :] < lengths[:, None]
    gain_one = norm1_gain.astype(f32)
    gain_two = norm2_gain.astype(f32)
    filled = jnp.where(masked, mask_embedding.astype(f32)[None, :], frames.astype(f32))
    first_norm, first_unit, first_inverse = norm_stats(filled, gain_one, norm1_bias.astype(f32))
    first_low = first_norm.astype(bf16)
    weight_flat = qkv_weight.reshape(model_width, 3 * local_width)
    bias_full = jnp.stack(
        [qv_bias[0].astype(f32), jnp.zeros((local_width,), f32), qv_bias[1].astype(f32)]
    ).reshape(3 * local_width)
    projected = (mm("rd,dc->rc", first_low, weight_flat) + bias_full).astype(bf16)
    triple = projected.reshape(utterances_here, frame_count, 3, heads_here, HEAD_DIM)
    queries = triple[:, :, 0]
    key_rows = triple[:, :, 1]
    values = triple[:, :, 2]
    mixture, log_total = lax.map(attend_forward, (queries, key_rows, values, key_valid))
    mixture_low = mixture.astype(bf16).reshape(row_count, local_width)
    mixture_all = lax.all_gather(mixture_low, "tensor", axis=1, tiled=True)
    out_all = lax.all_gather(out_weight, "tensor", axis=0, tiled=True)
    hidden = filled + mm("rl,ld->rd", mixture_all, out_all) + out_bias.astype(f32)
    second_norm, second_unit, second_inverse = norm_stats(hidden, gain_two, norm2_bias.astype(f32))
    second_low = second_norm.astype(bf16)
    up_rows = mm("rd,df->rf", second_low, up_weight) + up_bias.astype(f32)
    activ, gelu_pull = jax.vjp(partial(jax.nn.gelu, approximate=False), up_rows)
    activ_low = activ.astype(bf16)
    down_head = split(mm("fd,dv->fv", down_weight, head_weight))
    characters = head_weight.shape[1]
    own_logits = mm("rf,fv->rv", activ_low, down_head)
    own_logits = own_logits[:, :characters] + own_logits[:, characters:]
    hidden_down = (hidden + down_bias.astype(f32)).astype(bf16)
    logits = (
        lax.psum(own_logits, "tensor")
        + mm("rd,dv->rv", hidden_down, head_weight)
        + head_bias.astype(f32)
    )
    twice = jnp.concatenate([logit_grad, logit_grad], axis=1)
    grad_activ = mm("rv,fv->rf", twice, down_head)
    grad_up = gelu_pull(grad_activ)[0].astype(bf16)
    activ_head = mm("rf,rv->fv", activ_low, logit_grad)
    hidden_head = mm("rd,rv->dv", hidden_down, logit_grad)
    head_bias_grad = jnp.sum(logit_grad.astype(f32), axis=0)
    up_grad = mm("rd,rf->df", second_low, grad_up)
    up_bias_grad = jnp.sum(grad_up.astype(f32), axis=0)
    grad_second = mm("rf,df->rd", grad_up, up_weight)
    norm2_gain_grad = jnp.sum(grad_second * second_unit, axis=0)
    norm2_bias_grad = jnp.sum(grad_second, axis=0)
    grad_output = mm("rv,dv->rd", logit_grad, head_weight)
    grad_hidden = norm_back(grad_second, second_unit, second_inverse, gain_two) + jnp.where(
        first_share, grad_output, 0.0
    )
    grad_attn = grad_hidden.astype(bf16)
    out_bias_grad = jnp.sum(grad_hidden, axis=0)
    grad_mixture = lax.psum_scatter(
        mm("rd,ld->rl", grad_attn, out_all).astype(bf16), "tensor", scatter_dimension=1, tiled=True
    )
    out_grad = lax.psum_scatter(
        mm("rl,rd->ld", mixture_all, grad_attn).astype(bf16),
        "tensor",
        scatter_dimension=0,
        tiled=True,
    )
    grad_mixture = grad_mixture.reshape(utterances_here, frame_count, heads_here, HEAD_DIM)
    grad_queries, grad_keys, grad_values = lax.map(
        attend_backward, (queries, key_rows, values, key_valid, log_total, grad_mixture)
    )
    grad_triple = (
        jnp.stack([grad_queries, grad_keys, grad_values], axis=2)
        .astype(bf16)
        .reshape(row_count, 3 * local_width)
    )
    qkv_grad = mm("rd,rc->dc", first_low, grad_triple).reshape(model_width, 3, local_width)
    column_sums = jnp.sum(grad_triple.astype(f32), axis=0).reshape(3, local_width)
    qv_bias_grad = jnp.stack([column_sums[0], column_sums[2]])
    grad_first = mm("rc,dc->rd", grad_triple, weight_flat)
    norm1_gain_grad = jnp.sum(grad_first * first_unit, axis=0)
    norm1_bias_grad = jnp.sum(grad_first, axis=0)
    grad_filled = grad_hidden + norm_back(grad_first, first_unit, first_inverse, gain_one)
    mask_grad = jnp.sum(jnp.where(masked, grad_filled, 0.0), axis=0)
    frames_grad = jnp.where(masked, 0.0, grad_filled).astype(bf16)
    frames_grad = lax.all_gather(
        lax.psum_scatter(frames_grad, "tensor", scatter_dimension=0, tiled=True),
        "tensor",
        axis=0,
        tiled=True,
    ).astype(f32)
    up_grad = lax.psum(up_grad.astype(bf16), "dp").astype(f32)
    out_grad = lax.psum(out_grad, "dp").astype(f32)
    qkv_grad = lax.psum(qkv_grad.astype(bf16), "dp").astype(f32)
    activ_head, up_bias_grad, qv_bias_grad, head_bias_grad, hidden_head = lax.psum(
        (activ_head, up_bias_grad, qv_bias_grad, head_bias_grad, hidden_head), "dp"
    )
    activ_split = split(activ_head)
    head_twice = jnp.concatenate([head_weight, head_weight], axis=1)
    down_grad = mm("fv,dv->fd", activ_split, head_twice)
    down_head_grad = mm("fd,fv->dv", down_weight, activ_split)
    down_head_grad = down_head_grad[:, :characters] + down_head_grad[:, characters:]
    down_bias_grad = jnp.dot(
        head_weight.astype(f32), head_bias_grad, precision=lax.Precision.HIGHEST
    )
    mask_grad, norm1_gain_grad, norm1_bias_grad, norm2_gain_grad, norm2_bias_grad, out_bias_grad = (
        lax.psum(
            (
                mask_grad,
                norm1_gain_grad,
                norm1_bias_grad,
                norm2_gain_grad,
                norm2_bias_grad,
                out_bias_grad,
            ),
            ("dp", "tensor"),
        )
    )
    head_grad = hidden_head + lax.psum(down_head_grad, "tensor")
    return (
        logits,
        frames_grad,
        mask_grad,
        norm1_gain_grad,
        norm1_bias_grad,
        qkv_grad,
        qv_bias_grad,
        out_grad,
        out_bias_grad,
        norm2_gain_grad,
        norm2_bias_grad,
        up_grad,
        up_bias_grad,
        down_grad,
        down_bias_grad,
        head_grad,
        head_bias_grad,
    )


def solution(mesh):
    placed = (
        P("dp", None),
        P("dp"),
        P("dp", None),
        P(),
        P(),
        P(),
        P(None, None, "tensor"),
        P(None, "tensor"),
        P("tensor", None),
        P(),
        P(),
        P(),
        P(None, "tensor"),
        P("tensor"),
        P("tensor", None),
        P(),
        P(),
        P(),
        P("dp", None),
    )
    return jax.shard_map(
        local,
        mesh=mesh,
        in_specs=placed,
        out_specs=(
            P("dp", None),
            P("dp", None),
            P(),
            P(),
            P(),
            P(None, None, "tensor"),
            P(None, "tensor"),
            P("tensor", None),
            P(),
            P(),
            P(),
            P(None, "tensor"),
            P("tensor"),
            P("tensor", None),
            P(),
            P(),
            P(),
        ),
        check_vma=False,
    )
```

time: 765 us -> 612 us (0.80)
  waiting for transfers between devices: 391 us -> 243 us
  blocking collectives: 71.6 us -> 104 us
  other arithmetic: 87.8 us -> 60.7 us
  matrix products: 175 us -> 167 us
    psum x1 -> x3, waiting for transfers between devices: 181 us -> 89.4 us  [the longest x1 67.3 us: local(): qkv_grad = lax.psum(qkv_grad.astype(bf16), 'dp').astype(f32)]
    reduce_scatter x4 -> x3, waiting for transfers between devices: 136 us -> 69.5 us  [the longest x1 31.1 us: local(): lax.psum_scatter(frames_grad, 'tensor', scatter_dimension=0, tiled=True)]
    psum x1, blocking collectives: 8.13 us -> 42 us  [local(): lax.psum((mask_grad, norm1_gain_grad, norm1_bias_grad, norm2_gain_grad, n...]
    convert_element_type x24 -> x16, other arithmetic: 33.1 us -> 18.2 us  [the longest x1 5.64 us: local(): qkv_grad = lax.psum(qkv_grad.astype(bf16), 'dp').astype(f32)]
    all_gather x4 -> x3, waiting for transfers between devices: 72.8 us -> 82.8 us  [the longest x1 34.7 us: local(): out_all = lax.all_gather(out_weight, 'tensor', axis=0, tiled=True)]
    dot_general x15 -> x19, matrix products: 102 us -> 99.5 us  [the longest x18 98.7 us: mm(): return jnp.einsum(spec, left, right, preferred_element_type=f32)]
  transfers between devices with their start and end apart: 9 -> 9, of which waited for: 8 -> 9; matrix products, arithmetic and copies ran while one was open for 9% -> 24% of each run, Pallas kernels for 0% -> 0%
where the time goes in v1:
time: 612 us; the launch traced here: 604 us
  waiting for transfers between devices  243 us (40%)
  matrix products  167 us (27%)
  blocking collectives  104 us (17%)
  other arithmetic  60.7 us (10%)
  between operations  15.4 us (3%)
  local copies, waits for them, and re-layouts  13.7 us (2%)
    dot_general x18, matrix products, mm(): return jnp.einsum(spec, left, right, preferred_element_type=f32)  98.7 us
    psum x1, waiting for transfers between devices, local(): qkv_grad = lax.psum(qkv_grad.astype(bf16), 'dp').astype(f32)  67.3 us
    psum x1, blocking collectives, local(): lax.psum((activ_head, up_bias_grad, qv_bias_grad, head_bias_grad, hidden_...  61.9 us
    psum x1, blocking collectives, local(): lax.psum((mask_grad, norm1_gain_grad, norm1_bias_grad, norm2_gain_grad, n...  42 us
    all_gather x1, waiting for transfers between devices, local(): out_all = lax.all_gather(out_weight, 'tensor', axis=0, tiled=True)  34.7 us
    reduce_scatter x1, waiting for transfers between devices, local(): lax.psum_scatter(frames_grad, 'tensor', scatter_dimension=0, tiled=True)  31.1 us
    all_gather x1, waiting for transfers between devices, local(): mixture_all = lax.all_gather(mixture_low, 'tensor', axis=1, tiled=True)  28.1 us
    convert_element_type x1, other arithmetic, attend_backward(): grad_scores = (prob_rows * (grad_probs - row_dot)).astype(jnp.bfloat16)  22.6 us
  transfers between devices with their start and end apart: 9, of which 9 were waited for; matrix products, arithmetic and copies ran while one was open for 24% of the time, Pallas kernels for 0%

profile of v1, /device:TPU:0, one launch (start us, length us, event | category | flops | bytes accessed | tf_op | source)
XLA Modules:
  0.0 604.0 jit_solution(17303238965446216928)
XLA Ops:
  7.3 4.8 copy.54
  14.1 4.9 add_convert_fusion.1
  19.1 3.3 copy.55
  23.0 10.9 %fusion.46 = (f32[8,896]{1,0:T(8,128)S(1)}, f32[8,896,896]{1,2,0:T(8,128)}) fusion(bf16[1,896,3,8,64]{1,4,3,2,0:T(8,128)(2,1)S(1)} %bitcast.82, pred[896]{0:T(1024)(128)(4,1)S(1)} %iota_compare_fusion.2), kind=kOutput, calls=%fused_computation.116 | convolution fusion | flops 841344000 | bytes 27554816 | tf_op jit(solution)/shard_map/while/body/eval_jaxpr/qhd,khd->hqk/dot_general | solution.py:34
  34.0 10.3 %fusion = f32[8,896]{1,0:T(8,128)S(1)} fusion(f32[8,896,896]{1,2,0:T(8,128)} %get-tuple-element.108, f32[8,896]{1,0:T(8,128)S(1)} %get-tuple-element.107), kind=kLoop, calls=%fused_computation.6 | loop fusion | flops 12837888 | bytes 25747456 | tf_op jit(solution)/shard_map/while/body/eval_jaxpr/reduce_sum | solution.py:44
  44.4 11.6 %fusion.19 = bf16[8,64,896]{2,1,0:T(8,128)(2,1)} fusion(f32[8,896,896]{1,2,0:T(8,128)} %get-tuple-element.108, f32[8,896]{1,0:T(8,128)S(1)} %fusion, f32[8,896]{1,0:T(8,128)S(1)} %get-tuple-element.107, bf16[1,896,3,8,64]{1,4,3,2,0:T(8,128)(2,1)S(1)} %bitcast.83), kind=kOutput, calls=%fused_computation.61 | convolution fusion | flops 841809920 | bytes 27582464 | tf_op jit(solution)/shard_map/while/body/eval_jaxpr/hqk,khd->qhd/dot_general | solution.py:46
  57.4 3.5 fusion.44
  60.9 28.1 %all-gather.4.cloned.1.call-done = bf16[896,1024]{0,1:T(8,128)(2,1)} async-done(((bf16[896,512]{0,1:T(8,128)(2,1)}), bf16[896,1024]{0,1:T(8,128)(2,1)}) %all-gather.4.cloned.1.call-update) | async-done | bytes 1835024 | tf_op jit(solution)/shard_map/all_gather | solution.py:135
  89.0 34.7 %all-gather.6.cloned.1.call-done = bf16[1024,1024]{1,0:T(8,128)(2,1)} async-done(((bf16[512,1024]{1,0:T(8,128)(2,1)}), bf16[1024,1024]{1,0:T(8,128)(2,1)}) %all-gather.6.cloned.1.call-update) | async-done | bytes 2097168 | tf_op jit(solution)/shard_map/all_gather | solution.py:136
  123.7 5.5 fusion.47
  129.8 21.3 %multiply_convert_fusion.1 = (bf16[896,2048]{1,0:T(8,128)(2,1)}, f32[896,2048]{1,0:T(8,128)S(1)}, f32[896,2048]{1,0:T(8,128)S(1)}) fusion(f32[2048]{0:T(1024)S(1)} %convert_element_type.181, bf16[1024,2048]{1,0:T(8,128)(2,1)S(1)} %copy-done.41, f32[896,1024]{1,0:T(8,128)S(1)} %get-tuple-element.110, f32[1024]{0:T(1024)S(1)} %convert_element_type.179, ...), kind=kOutput, calls=%fused_computation.15 | convolution fusion | flops 3883794432 | bytes 26237952 | tf_op jit(solution)/shard_map/rd,df->rf/dot_general | solution.py:107
  151.1 5.3 convert_reduce_fusion
  156.4 6.7 %multiply_reduce_fusion.1 = (f32[1024]{0:T(1024)S(1)}, f32[896]{0:T(1024)S(1)}, f32[896]{0:T(1024)S(1)}, f32[1024]{0:T(1024)S(1)}, f32[896,1024]{1,0:T(8,128)S(1)}) fusion(f32[896,1024]{1,0:T(8,128)S(1)} %get-tuple-element.110, f32[896]{0:T(1024)S(1)} %add_rsqrt_fusion, f32[896]{0:T(1024)S(1)} %broadcast_multiply_fusion.4, ...), kind=kOutput, calls=%fused_computation.33 | convolution fusion | flops 3766349824 | bytes 15230976 | tf_op jit(solution)/shard_map/rf,df->rd/dot_general | solution.py:107
  163.2 1.5 select_add_fusion
  164.7 1.8 copy-done.7
  166.5 3.4 convolution_convert_fusion.3
  170.1 3.3 fusion.24
  173.3 1.5 fusion.48
  174.9 6.9 %convolution_convert_fusion.2 = bf16[1024,1024]{1,0:T(8,128)(2,1)} fusion(bf16[896,1024]{0,1:T(8,128)(2,1)} %all-gather.4.cloned.1.call-done, f32[896,1024]{1,0:T(8,128)} %copy-done.7), kind=kOutput, calls=%fused_computation.55 | convolution fusion | flops 1881014272 | bytes 7602176 | tf_op jit(solution)/shard_map/rl,rd->ld/dot_general | solution.py:107
  181.8 17.2 %reduce-scatter.4.cloned.1.call-done = bf16[896,512]{1,0:T(8,128)(2,1)} async-done(((bf16[896,1024]{1,0:T(8,128)(2,1)}), bf16[896,512]{1,0:T(8,128)(2,1)}) %reduce-scatter.4.cloned.1.call-update) | async-done | bytes 917520 | tf_op jit(solution)/shard_map/reduce_scatter | solution.py:170
  199.1 2.2 copy.57
  201.3 16.7 %multiply_reduce_fusion = (f32[8,896]{1,0:T(8,128)S(1)}, f32[8,896,896]{1,2,0:T(8,128)}) fusion(f32[8,896,896]{1,2,0:T(8,128)} %get-tuple-element.108, f32[8,896]{1,0:T(8,128)S(1)} %log_add_fusion, bf16[896,8,64]{0,2,1:T(8,128)(2,1)} %bitcast.87, bf16[1,896,3,8,64]{1,4,3,2,0:T(8,128)(2,1)S(1)} %bitcast.84), kind=kOutput, calls=%fused_computation.1 | convolution fusion | flops 841344000 | bytes 53272576 | tf_op jit(solution)/shard_map/while/body/eval_jaxpr/qhd,khd->hqk/dot_general | solution.py:61
  218.0 22.6 %multiply_convert_fusion = bf16[8,896,896]{1,2,0:T(8,128)(2,1)} fusion(f32[8,896,896]{1,2,0:T(8,128)} %get-tuple-element.114, f32[8,896,896]{1,2,0:T(8,128)} %get-tuple-element.108, f32[8,896]{1,0:T(8,128)S(1)} %get-tuple-element.113, f32[8,896]{1,0:T(8,128)S(1)} %log_add_fusion), kind=kLoop, calls=%fused_computation | loop fusion | flops 25690112 | bytes 64282624 | tf_op jit(solution)/shard_map/while/body/eval_jaxpr/convert_element_type | solution.py:65
  240.6 10.1 %multiply_bitcast_fusion = bf16[1,896,1,8,64]{1,4,3,2,0:T(8,128)(2,1)} fusion(bf16[8,896,896]{1,2,0:T(8,128)(2,1)} %multiply_convert_fusion, bf16[1,896,3,8,64]{1,4,3,2,0:T(8,128)(2,1)} %bitcast.85), kind=kOutput, calls=%fused_computation.57 | convolution fusion | flops 823001088 | bytes 14680064 | tf_op jit(solution)/shard_map/while/body/eval_jaxpr/hqk,qhd->khd/dot_general | solution.py:71
  250.7 4.3 multiply_bitcast_fusion.1
  255.0 13.8 %fusion.16 = bf16[1,896,1,8,64]{1,4,3,2,0:T(8,128)(2,1)} fusion(bf16[896,8,64]{0,2,1:T(8,128)(2,1)} %bitcast.88, f32[8,896,896]{1,2,0:T(8,128)} %get-tuple-element.108, f32[8,896]{1,0:T(8,128)S(1)} %log_add_fusion), kind=kOutput, calls=%fused_computation.60 | convolution fusion | flops 834928640 | bytes 27553792 | tf_op jit(solution)/shard_map/while/body/eval_jaxpr/hqk,qhd->khd/dot_general | solution.py:55
  268.9 2.1 convert_reduce_fusion.1
  271.9 4.4 multiply_reduce_fusion.2
  276.3 2.4 select_reduce_fusion
  278.7 1.7 select_convert_fusion
  280.5 3.4 fusion.28
  284.6 8.6 %convolution_convert_fusion = bf16[1024,2048]{1,0:T(8,128)(2,1)} fusion(bf16[896,2048]{1,0:T(8,128)(2,1)} %get-tuple-element.117, f32[896,1024]{1,0:T(8,128)S(1)} %copy-done.2, f32[1024]{0:T(1024)S(1)} %convert_element_type.179, f32[1024]{0:T(1024)S(1)} %convert_element_type.178, f32[896]{0:T(1024)S(1)} %add_rsqrt_fusion, f32[896]{0:T(1024)S(1)} %broadcast_multiply_fusion.4), kind=kOutput, calls=%fused_computation.32 | convolution fusion | flops 3764781056 | bytes 11549696 | tf_op jit(solution)/shard_map/rd,rf->df/dot_general | solution.py:107
  294.6 3.0 convolution_bitcast_fusion
  298.4 7.5 %convolution_convert_fusion.1 = bf16[1024,3,512]{2,0,1:T(8,128)(2,1)} fusion(bf16[3,512,896]{2,1,0:T(8,128)(2,1)} %bitcast.92, bf16[896,1024]{1,0:T(8,128)(2,1)S(1)} %copy-done.6, f32[1024]{0:T(1024)S(1)} %copy-done.31, f32[1024]{0:T(1024)S(1)} %copy-done.25, f32[896]{0:T(1024)S(1)} %copy-done.27, f32[896]{0:T(1024)S(1)} %copy-done.23, ...), kind=kOutput, calls=%fused_computation.54 | convolution fusion | flops 2826567680 | bytes 7753600 | tf_op jit(solution)/shard_map/rd,rc->dc/dot_general | solution.py:107
  305.9 21.2 %reduce-scatter.8.cloned.1.call-done = bf16[512,1024]{1,0:T(8,128)(2,1)} async-done(((bf16[1024,1024]{1,0:T(8,128)(2,1)}), bf16[512,1024]{1,0:T(8,128)(2,1)}) %reduce-scatter.8.cloned.1.call-update) | async-done | bytes 1048592 | tf_op jit(solution)/shard_map/reduce_scatter | solution.py:173
  327.2 31.1 %reduce-scatter.6.cloned.1.call-done = bf16[448,1024]{1,0:T(8,128)(2,1)} async-done(((bf16[896,1024]{1,0:T(8,128)(2,1)}), bf16[448,1024]{1,0:T(8,128)(2,1)}) %reduce-scatter.6.cloned.1.call-update) | async-done | bytes 917520 | tf_op jit(solution)/shard_map/reduce_scatter | solution.py:198
  358.4 4.7 fusion.27
  363.1 21.8 %all-reduce.11.cloned.1.call-done = (f32[896,32]{0,1:T(8,128)}, f32[1024,32]{0,1:T(8,128)}) async-done(((f32[896,32]{0,1:T(8,128)}, f32[1024,32]{0,1:T(8,128)}), (f32[896,32]{0,1:T(8,128)}, f32[1024,32]{0,1:T(8,128)})) %all-reduce.11.cloned.1.call-update) | async-done | bytes 245776 | tf_op jit(solution)/shard_map/psum | solution.py:149
  384.9 1.6 add.183
  386.5 3.4 fusion.20
  390.0 42.0 %all-reduce = (f32[1024]{0:T(1024)}, f32[1024]{0:T(1024)}, f32[1024]{0:T(1024)}, f32[1024]{0:T(1024)}, f32[1024]{0:T(1024)}, /*index=5*/f32[1024]{0:T(1024)}) all-reduce(f32[1024]{0:T(1024)S(1)} %get-tuple-element.94, f32[1024]{0:T(1024)S(1)} %get-tuple-element.70, ...), channel_id=1, replica_groups=mesh['dp'=16,'tensor'=2] {'dp','tensor'}, use_global_device_ids=true, to_apply=%region_16.17 | all-reduce | flops 6144 | bytes 49152 | tf_op jit(solution)/shard_map/psum | solution.py:218
  431.9 61.9 %all-reduce.1 = (f32[2,512]{1,0:T(2,128)}, f32[2048]{0:T(1024)}, f32[32]{0:T(128)S(1)}) all-reduce(f32[2,512]{1,0:T(2,128)S(1)} %pad_maximum_fusion.7, f32[2048]{0:T(1024)S(1)} %get-tuple-element.116, f32[32]{0:T(128)S(1)} %convert_reduce_fusion.2), channel_id=1, replica_groups=mesh['dp'=16,'tensor'=2] {'dp'}, use_global_device_ids=true, to_apply=%region_23.24 | all-reduce | flops 3104 | bytes 24832 | tf_op jit(solution)/shard_map/psum | solution.py:206
  494.6 67.3 %all-reduce.13.cloned.1.call-done = (bf16[1024,3,512]{2,0,1:T(8,128)(2,1)}, bf16[512,1024]{1,0:T(8,128)(2,1)}, bf16[1024,2048]{1,0:T(8,128)(2,1)}) async-done(((bf16[1024,3,512]{2,0,1:T(8,128)(2,1)}, bf16[512,1024]{1,0:T(8,128)(2,1)}, bf16[1024,2048]{1,0:T(8,128)(2,1)}), (bf16[1024,3,512]{2,0,1:T(8,128)(2,1)}, bf16[512,1024]{1,0:T(8,128)(2,1)}, bf16[1024,2048]{1,0:T(8,128)(2,1)})) %all-reduce.13.cloned.1.call-update) | async-done | bytes 8388624 | tf_op jit(solution)/shard_map/psum | solution.py:205
  561.9 5.6 convert_element_type.199
  567.5 1.6 convert_element_type.202
  569.1 4.4 convert_element_type.204
  573.5 20.0 %all-gather.8.cloned.1.call-done = bf16[896,1024]{1,0:T(8,128)(2,1)} async-done(((bf16[448,1024]{1,0:T(8,128)(2,1)}), bf16[896,1024]{1,0:T(8,128)(2,1)}) %all-gather.8.cloned.1.call-update) | async-done | bytes 1835024 | tf_op jit(solution)/shard_map/all_gather | solution.py:197
  593.5 3.7 convert_element_type.197
  (142 shorter events, 9.0 us)
Async XLA Ops:
  7.2 4.9 copy-start.28
  7.2 5.0 copy-start.32
  7.2 5.0 copy-start.33
  7.2 5.1 copy-start.34
  7.2 5.1 copy-start.40
  7.2 5.2 copy-start.5
  7.3 81.8 %all-gather.4.cloned.1.call-start = ((), (), s32[]{:S(2)}) async-start(), calls=%async_computation.3 | async-start | bytes 2752512 | tf_op jit(solution)/shard_map/all_gather | solution.py:135
  12.2 1.9 copy-start.11
  12.3 6.8 %copy-start.24 = (f32[1024]{0:T(1024)}, f32[1024]{0:T(1024)S(1)}, u32[]{:S(2)}) copy-start(f32[1024]{0:T(1024)S(1)} %convert_element_type.168) | copy-start | bytes 12292
  13.9 5.2 copy-start.26
  22.4 178.9 %copy-start.3 = (bf16[896,1536]{0,1:T(8,128)(2,1)}, bf16[896,1536]{0,1:T(8,128)(2,1)S(1)}, u32[]{:S(2)}) copy-start(bf16[896,1536]{0,1:T(8,128)(2,1)S(1)} %copy.55) | copy-start | bytes 8257540
  44.3 13.0 %copy-start.29 = (bf16[2048]{0:T(1024)(128)(2,1)S(1)}, bf16[2048]{0:T(1024)(128)(2,1)}, u32[]{:S(2)}) copy-start(bf16[2048]{0:T(1024)(128)(2,1)} %param.32) | copy-start | bytes 12292
  44.3 13.0 %copy-start.35 = (bf16[1024]{0:T(1024)(128)(2,1)S(1)}, bf16[1024]{0:T(1024)(128)(2,1)}, u32[]{:S(2)}) copy-start(bf16[1024]{0:T(1024)(128)(2,1)} %param.28) | copy-start | bytes 6148
  44.3 13.0 %copy-start.36 = (bf16[1024]{0:T(1024)(128)(2,1)S(1)}, bf16[1024]{0:T(1024)(128)(2,1)}, u32[]{:S(2)}) copy-start(bf16[1024]{0:T(1024)(128)(2,1)} %param.30) | copy-start | bytes 6148
  44.3 13.0 %copy-start.37 = (bf16[1024]{0:T(1024)(128)(2,1)S(1)}, bf16[1024]{0:T(1024)(128)(2,1)}, u32[]{:S(2)}) copy-start(bf16[1024]{0:T(1024)(128)(2,1)} %param.29) | copy-start | bytes 6148
  44.3 13.0 %copy-start.14 = (bf16[1024,32]{0,1:T(8,128)(2,1)S(1)}, bf16[1024,32]{0,1:T(8,128)(2,1)}, u32[]{:S(2)}) copy-start(bf16[1024,32]{0,1:T(8,128)(2,1)} %param.35) | copy-start | bytes 196612
  56.0 67.7 %all-gather.6.cloned.1.call-start = ((), (), s32[]{:S(2)}) async-start(), calls=%async_computation.4 | async-start | bytes 3145728 | tf_op jit(solution)/shard_map/all_gather | solution.py:136
  56.8 142.3 %reduce-scatter.4.cloned.1.call-start = ((), (), s32[]{:S(2)}) async-start(), calls=%async_computation.5 | async-start | bytes 2752512 | tf_op jit(solution)/shard_map/reduce_scatter | solution.py:170
  60.9 90.1 %copy-start.17 = (bf16[2048,32]{0,1:T(8,128)(2,1)}, bf16[2048,32]{0,1:T(8,128)(2,1)S(1)}, u32[]{:S(2)}) copy-start(bf16[2048,32]{0,1:T(8,128)(2,1)S(1)} %get-tuple-element.101) | copy-start | bytes 393220
  60.9 90.1 %copy-start.19 = (bf16[2048,32]{0,1:T(8,128)(2,1)}, bf16[2048,32]{0,1:T(8,128)(2,1)S(1)}, u32[]{:S(2)}) copy-start(bf16[2048,32]{0,1:T(8,128)(2,1)S(1)} %get-tuple-element.102) | copy-start | bytes 393220
  123.7 6.0 copy-start.41
  129.2 34.0 %copy-start.1 = (f32[896,1024]{1,0:T(8,128)}, f32[896,1024]{1,0:T(8,128)S(1)}, u32[]{:S(2)}) copy-start(f32[896,1024]{1,0:T(8,128)S(1)} %get-tuple-element.110) | copy-start | bytes 11010052
  129.7 21.3 %copy-start.16 = (bf16[896,32]{0,1:T(8,128)(2,1)S(1)}, bf16[896,32]{0,1:T(8,128)(2,1)}, u32[]{:S(2)}) copy-start(bf16[896,32]{0,1:T(8,128)(2,1)} %param.37) | copy-start | bytes 172036
  163.2 3.4 copy-start.42
  166.5 3.5 copy-start.38
  169.9 123.6 %all-reduce.9.cloned.1.call-start = ((), (), s32[]{:S(2)}) async-start(), calls=%async_computation.9 | async-start | bytes 786432 | tf_op jit(solution)/shard_map/psum | solution.py:206
  170.0 3.3 copy-start.4
  174.8 152.3 %reduce-scatter.8.cloned.1.call-start = ((), (), s32[]{:S(2)}) async-start(), calls=%async_computation.8 | async-start | bytes 3145728 | tf_op jit(solution)/shard_map/reduce_scatter | solution.py:173
  181.8 176.5 %reduce-scatter.6.cloned.1.call-start = ((), (), s32[]{:S(2)}) async-start(), calls=%async_computation.6 | async-start | bytes 2752512 | tf_op jit(solution)/shard_map/reduce_scatter | solution.py:198
  240.6 10.1 %copy-start = (bf16[8,896,896]{1,2,0:T(8,128)(2,1)S(1)}, bf16[8,896,896]{1,2,0:T(8,128)(2,1)}, u32[]{:S(2)}) copy-start(bf16[8,896,896]{1,2,0:T(8,128)(2,1)} %multiply_convert_fusion) | copy-start | bytes 38535172
  255.0 13.8 %copy-start.10 = (bf16[1,896,1,8,64]{1,4,3,2,0:T(8,128)(2,1)S(1)}, bf16[1,896,1,8,64]{1,4,3,2,0:T(8,128)(2,1)}, u32[]{:S(2)}) copy-start(bf16[1,896,1,8,64]{1,4,3,2,0:T(8,128)(2,1)} %multiply_bitcast_fusion) | copy-start | bytes 2752516
  268.8 2.1 copy-start.6
  268.8 3.0 copy-start.12
  268.8 3.0 copy-start.23
  268.9 3.0 copy-start.25
  268.9 3.0 copy-start.27
  271.0 5.3 copy-start.13
  271.9 4.4 copy-start.8
  280.5 104.4 %all-reduce.11.cloned.1.call-start = ((), (), s32[]{:S(2)}) async-start(), calls=%async_computation.10 | async-start | bytes 491520 | tf_op jit(solution)/shard_map/psum | solution.py:149
  280.5 4.1 copy-start.2
  293.2 5.2 copy-start.31
  298.4 263.5 %all-reduce.13.cloned.1.call-start = ((), (), s32[]{:S(2)}) async-start(), calls=%async_computation.11 | async-start | bytes 16777216 | tf_op jit(solution)/shard_map/psum | solution.py:205
  327.1 31.2 %copy-start.43 = (bf16[32]{0:T(256)(128)(2,1)S(1)}, bf16[32]{0:T(256)(128)(2,1)}, u32[]{:S(2)}) copy-start(bf16[32]{0:T(256)(128)(2,1)} %param.36) | copy-start | bytes 196
  327.1 266.4 %all-gather.8.cloned.1.call-start = ((), (), s32[]{:S(2)}) async-start(), calls=%async_computation.7 | async-start | bytes 2752512 | tf_op jit(solution)/shard_map/all_gather | solution.py:197
  358.4 26.4 %copy-start.21 = (f32[1024,32]{0,1:T(8,128)S(1)}, f32[1024,32]{0,1:T(8,128)}, u32[]{:S(2)}) copy-start(f32[1024,32]{0,1:T(8,128)} %get-tuple-element.86) | copy-start | bytes 393220
  493.8 73.7 %copy-start.39 = (f32[32]{0:T(128)}, f32[32]{0:T(128)S(1)}, u32[]{:S(2)}) copy-start(f32[32]{0:T(128)S(1)} %get-tuple-element.84) | copy-start | bytes 388
  561.9 5.6 copy-start.15
  561.9 7.2 %copy-start.9 = (bf16[1024,2048]{1,0:T(8,128)(2,1)S(1)}, bf16[1024,2048]{1,0:T(8,128)(2,1)}, u32[]{:S(2)}) copy-start(bf16[1024,2048]{1,0:T(8,128)(2,1)} %get-tuple-element.91) | copy-start | bytes 12582916
  (5 other events, 7.9 us)
Sparse Core Ops, SparseCore 0:
  56.1 32.8 all-gather.3
  90.6 33.1 all-gather.5
  170.1 28.9 reduce-scatter.3
  202.8 90.7 all-reduce.8
  296.2 30.8 reduce-scatter.7
  329.3 28.9 reduce-scatter.5
  361.8 23.0 all-reduce.10
  389.5 172.3 all-reduce.12
  563.5 29.9 all-gather.7
